TPU v7x, 32 devices: a whole 2x2x4 slice. The times are simulated.
32 devices in a mesh: dp: 8 (over z, core), seq: 4 (over y, x).
Axes of the slice: x: 2, y: 2, z: 4, core: 2. Of those that a mesh axis runs over, the one named last changes fastest.
Arguments:
- queries: bfloat16 [8, 4, 144, 1536], P('dp', 'seq'), may hold values from -32 to 32
- keys: bfloat16 [8, 4, 144, 1536], P('dp', 'seq'), may hold values from -32 to 32
- values: bfloat16 [8, 4, 144, 1536], P('dp', 'seq'), may hold values from -6 to 6
- cotangent: bfloat16 [8, 4, 144, 1536], P('dp', 'seq'), may hold values from -6 to 6
- spatial_count: int32 [8, 4], P('dp', 'seq'), may hold values from 72 to 144, as said below
- clip_ids: int32 [8, 4], P('dp'), may hold values from 0 to 1, never falling along the last dimension, each value on 1 to 3 neighbouring positions
- time_bias: float32 [12, 4], replicated, may hold values from -4 to 4
Outputs:
- attended: bfloat16 [8, 4, 144, 1536], P('dp', 'seq')
- query_grad: bfloat16 [8, 4, 144, 1536], P('dp', 'seq')
- key_grad: bfloat16 [8, 4, 144, 1536], P('dp', 'seq')
- value_grad: bfloat16 [8, 4, 144, 1536], P('dp', 'seq')
- bias_grad: float32 [12, 4], replicated
Inputs may be any that keep to these rules, and one draw needn't show every extreme that they name: The live spatial tokens of a frame are its first spatial_count positions; in each group some frame has all 144 live. `clip_ids`: frames of one clip are consecutive; a clip has at most 3 frames.
All inputs are finite; a program needn't handle non-finite values.
Results may differ from a plain program's by a relative error of at most 0.0059.
Values may be sent and summed in bfloat16 or wider, within the bound.
A program may use at most 64 MiB of HBM per device.

v0:
```python
import functools
import math

import jax
import jax.numpy as jnp
from jax import lax
from jax.experimental import pallas as pl
from jax.experimental.pallas import tpu as pltpu
from jax.sharding import PartitionSpec as P

SPACE_PATTERNS = ("bfihe,bfjhe->bfhij", "bfhij,bfjhe->bfihe", "bfhij,bfihe->bfjhe")
TIME_PATTERNS = ("biphe,bjphe->bphij", "bphij,bjphe->biphe", "bphij,biphe->bjphe")


def split_heads(tensor, head_count):
    return tensor.reshape(tensor.shape[:-1] + (head_count, tensor.shape[-1] // head_count))


def join_heads(tensor):
    return tensor.reshape(tensor.shape[:-2] + (tensor.shape[-2] * tensor.shape[-1],))


def attend_forward(patterns, query_part, key_part, value_part, bias, allowed):
    scaling = 1.0 / math.sqrt(query_part.shape[-1])
    scores = (
        jnp.einsum(patterns[0], query_part, key_part, preferred_element_type=jnp.float32) * scaling
        + bias
    )
    scores = jnp.where(allowed, scores, -1e30)
    row_peak = jnp.max(scores, axis=-1, keepdims=True)
    weights = jnp.exp(scores - row_peak)
    shares = weights / jnp.sum(weights, axis=-1, keepdims=True)
    shares_half = shares.astype(jnp.bfloat16)
    result = jnp.einsum(patterns[1], shares_half, value_part, preferred_element_type=jnp.float32)
    return (shares, shares_half, result)


def attend_backward(
    patterns, query_part, key_part, value_part, cotangent_part, shares, shares_half
):
    scaling = 1.0 / math.sqrt(query_part.shape[-1])
    value_grad = jnp.einsum(
        patterns[2], shares_half, cotangent_part, preferred_element_type=jnp.float32
    )
    share_grad = jnp.einsum(
        patterns[0], cotangent_part, value_part, preferred_element_type=jnp.float32
    )
    spread = jnp.sum(shares * share_grad, axis=-1, keepdims=True)
    score_grad = shares * (share_grad - spread)
    score_half = score_grad.astype(jnp.bfloat16)
    query_grad = (
        jnp.einsum(patterns[1], score_half, key_part, preferred_element_type=jnp.float32) * scaling
    )
    key_grad = (
        jnp.einsum(patterns[2], score_half, query_part, preferred_element_type=jnp.float32)
        * scaling
    )
    return (query_grad, key_grad, value_grad, score_grad)


def on_device(queries, keys, values, cotangent, spatial_count, clip_ids, time_bias):
    head_count, frames_all = time_bias.shape
    positions = queries.shape[2]
    row_index = lax.broadcasted_iota(jnp.int32, (frames_all, frames_all), 0)
    col_index = lax.broadcasted_iota(jnp.int32, (frames_all, frames_all), 1)
    distance = jnp.abs(row_index - col_index)
    lag_index = lax.broadcasted_iota(jnp.int32, (frames_all, frames_all, frames_all), 0)
    onehot = (lag_index == distance[None]).astype(jnp.float32)
    bias_table = jnp.tensordot(time_bias, onehot, axes=1, precision=lax.Precision.HIGHEST)[
        None, None
    ]
    same_clip = (clip_ids[:, :, None] == clip_ids[:, None, :])[:, None, None]
    position = lax.broadcasted_iota(jnp.int32, (1, 1, 1, 1, positions), 4)
    live_keys = position < spatial_count[:, :, None, None, None]
    space_query = split_heads(queries, head_count)
    space_key = split_heads(keys, head_count)
    space_value = split_heads(values, head_count)
    space_slope = split_heads(cotangent, head_count)
    space_shares, space_half, space_out = attend_forward(
        SPACE_PATTERNS, space_query, space_key, space_value, 0.0, live_keys
    )
    space_grads = attend_backward(
        SPACE_PATTERNS, space_query, space_key, space_value, space_slope, space_shares, space_half
    )
    query_rows, key_rows, value_rows = (
        lax.all_to_all(queries, "seq", split_axis=2, concat_axis=1, tiled=True),
        lax.all_to_all(keys, "seq", split_axis=2, concat_axis=1, tiled=True),
        lax.all_to_all(values, "seq", split_axis=2, concat_axis=1, tiled=True),
    )
    query_part = split_heads(query_rows, head_count)
    key_part = split_heads(key_rows, head_count)
    value_part = split_heads(value_rows, head_count)
    shares, shares_half, result = attend_forward(
        TIME_PATTERNS, query_part, key_part, value_part, bias_table, same_clip
    )
    held = (query_part, key_part, value_part)
    back_out = lax.all_to_all(
        join_heads(result).astype(jnp.bfloat16), "seq", split_axis=1, concat_axis=2, tiled=True
    )
    slope_rows = lax.all_to_all(cotangent, "seq", split_axis=2, concat_axis=1, tiled=True)
    slope_part = split_heads(slope_rows, head_count)
    time_grads = attend_backward(
        TIME_PATTERNS, held[0], held[1], held[2], slope_part, shares, shares_half
    )
    qgrad_rows = join_heads(time_grads[0]).astype(jnp.bfloat16)
    kgrad_rows = join_heads(time_grads[1]).astype(jnp.bfloat16)
    vgrad_rows = join_heads(time_grads[2]).astype(jnp.bfloat16)
    back_query, back_key, back_value = (
        lax.all_to_all(qgrad_rows, "seq", split_axis=1, concat_axis=2, tiled=True),
        lax.all_to_all(kgrad_rows, "seq", split_axis=1, concat_axis=2, tiled=True),
        lax.all_to_all(vgrad_rows, "seq", split_axis=1, concat_axis=2, tiled=True),
    )
    attended = (join_heads(space_out) + back_out.astype(jnp.float32)).astype(jnp.bfloat16)
    query_grad = (join_heads(space_grads[0]) + back_query.astype(jnp.float32)).astype(jnp.bfloat16)
    key_grad = (join_heads(space_grads[1]) + back_key.astype(jnp.float32)).astype(jnp.bfloat16)
    value_grad = (join_heads(space_grads[2]) + back_value.astype(jnp.float32)).astype(jnp.bfloat16)
    bias_part = jnp.tensordot(
        jnp.sum(time_grads[3], axis=(0, 1)),
        onehot,
        axes=((1, 2), (1, 2)),
        precision=lax.Precision.HIGHEST,
    )
    summed = lax.psum(bias_part, ("dp", "seq"))
    bias_grad = summed / math.sqrt(lax.axis_size("dp") * queries.shape[0] * frames_all * positions)
    return (attended, query_grad, key_grad, value_grad, bias_grad)


ROWS = 16
MESH = pl.DeviceIdType.MESH
NT = (((1,), (1,)), ((), ()))
NN = (((1,), (0,)), ((), ()))
TN = (((0,), (0,)), ((), ()))


def dot(left, right, dims):
    return lax.dot_general(left, right, dims, preferred_element_type=jnp.float32)


def attend_block(query, key, value, slope, extra, scaling):
    scores = dot(query, key, NT) * scaling + extra
    share_grad = dot(slope, value, NT)
    weights = jnp.exp(scores - jnp.max(scores, axis=-1, keepdims=True))
    shares = weights * (1.0 / jnp.sum(weights, axis=-1, keepdims=True))
    shares_half = shares.astype(jnp.bfloat16)
    spread = jnp.sum(shares * share_grad, axis=-1, keepdims=True)
    score_grad = shares * (share_grad - spread)
    score_half = score_grad.astype(jnp.bfloat16)
    grads = (
        dot(shares_half, value, NN),
        dot(score_half, key, NN) * scaling,
        dot(score_half, query, TN) * scaling,
        dot(shares_half, slope, TN),
    )
    return grads, score_grad


def partner(count, me, off, back=False):
    if count & (count - 1):
        return lax.rem(me + (count - off if back else off), count)
    other, bit = 0, 1
    while bit < count:
        mine = lax.rem(me // bit, 2)
        other = other + bit * (1 - mine if off & bit else mine)
        bit *= 2
    return other


def kernel(
    dp, n, heads, bias_scale,
    q_ref, k_ref, v_ref, c_ref, count_ref, clip_ref, bias_ref,
    out_ref, qg_ref, kg_ref, vg_ref, bg_ref,
    held, rx, res, ret, space, bx, by,
    load_sem, own_sem, fs, fr, bs, br, xs, xr, ys, yr,
):
    ins = (q_ref, k_ref, v_ref, c_ref)
    outs = (out_ref, qg_ref, kg_ref, vg_ref)
    rows, width = q_ref.shape
    size = width // heads
    per = heads // n
    scaling = 1.0 / math.sqrt(size)
    me = lax.axis_index("seq")
    me_dp = lax.axis_index("dp")

    def cols(index):
        return pl.ds(pl.multiple_of(index * size, size), size)

    def load(a):
        return pltpu.make_async_copy(ins[a], held.at[a], load_sem.at[a])

    def own(a):
        mine = pl.ds(pl.multiple_of(me * per * size, size), per * size)
        return pltpu.make_async_copy(ins[a].at[:, mine], rx.at[a, me], own_sem.at[a])

    def forth(r, a, off, slot):
        to = partner(n, me, off)
        return pltpu.make_async_remote_copy(
            src_ref=ins[a].at[:, cols(to * per + r)],
            dst_ref=rx.at[a, slot, :, cols(r)],
            send_sem=fs.at[r, a, off - 1],
            recv_sem=fr.at[r, a, off - 1],
            device_id={"seq": to},
            device_id_type=MESH,
        )

    def back(r, a, off, slot):
        to = partner(n, me, off)
        return pltpu.make_async_remote_copy(
            src_ref=res.at[a, to, :, cols(r)],
            dst_ref=ret.at[a, :, cols(slot * per + r)],
            send_sem=bs.at[r, a, off - 1],
            recv_sem=br.at[r, a, off - 1],
            device_id={"seq": to},
            device_id_type=MESH,
        )

    def bias_dp(off, slot):
        return pltpu.make_async_remote_copy(
            src_ref=bx.at[me_dp],
            dst_ref=bx.at[slot],
            send_sem=xs.at[off - 1],
            recv_sem=xr.at[off - 1],
            device_id={"dp": partner(dp, me_dp, off)},
            device_id_type=MESH,
        )

    def bias_seq(off, slot):
        return pltpu.make_async_remote_copy(
            src_ref=by.at[me],
            dst_ref=by.at[slot],
            send_sem=ys.at[off - 1],
            recv_sem=yr.at[off - 1],
            device_id={"seq": partner(n, me, off)},
            device_id_type=MESH,
        )

    for a in range(4):
        load(a).start()
        own(a).start()
    barrier = pltpu.get_barrier_semaphore()
    for off in range(1, n):
        pl.semaphore_signal(
            barrier, inc=1, device_id={"seq": partner(n, me, off)}, device_id_type=MESH
        )
    for off in range(1, dp):
        pl.semaphore_signal(
            barrier, inc=1, device_id={"dp": partner(dp, me_dp, off)}, device_id_type=MESH
        )
    pl.semaphore_wait(barrier, n - 1 + dp - 1)

    for r in range(per):
        for a in range(4):
            for off in range(n - 1, 0, -1):
                forth(r, a, off, me).start()

    tokens = n * ROWS
    row = lax.broadcasted_iota(jnp.int32, (tokens, tokens), 0)
    col = lax.broadcasted_iota(jnp.int32, (tokens, tokens), 1)
    row_frame, col_frame = row // ROWS, col // ROWS
    distance = jnp.abs(row_frame - col_frame)
    row_clip = jnp.zeros((tokens, tokens), jnp.int32)
    col_clip = jnp.zeros((tokens, tokens), jnp.int32)
    for f in range(n):
        row_clip = jnp.where(row_frame == f, clip_ref[0, f], row_clip)
        col_clip = jnp.where(col_frame == f, clip_ref[0, f], col_clip)
    allowed = (row_clip == col_clip) & (row - row_frame * ROWS == col - col_frame * ROWS)
    live = lax.broadcasted_iota(jnp.int32, (rows, rows), 1) < count_ref[0, 0]
    space_extra = jnp.where(live, 0.0, -1e30)
    lane = lax.broadcasted_iota(jnp.int32, (8, 128), 1)
    line = lax.broadcasted_iota(jnp.int32, (8, 128), 0)

    for a in range(4):
        load(a).wait()
        own(a).wait()
    bx[me_dp] = jnp.zeros((8, 128), jnp.float32)

    def spatial(h):
        parts = [held[a, :, cols(h)] for a in range(4)]
        grads, _ = attend_block(*parts, space_extra, scaling)
        for a in range(4):
            space[a, :, cols(h)] = grads[a]

    def temporal(r):
        head = me * per + r
        bias = jnp.zeros((tokens, tokens), jnp.float32)
        for d in range(n):
            bias = jnp.where(distance == d, bias_ref[head, d], bias)
        extra = jnp.where(allowed, bias, -1e30)
        total = jnp.zeros((tokens, tokens), jnp.float32)
        for b in range(rows // ROWS):
            span = pl.ds(b * ROWS, ROWS)
            parts = [
                jnp.concatenate([rx[a, f, span, cols(r)] for f in range(n)], axis=0)
                for a in range(4)
            ]
            grads, score_grad = attend_block(*parts, extra, scaling)
            total = total + score_grad
            for a in range(4):
                half = grads[a].astype(jnp.bfloat16)
                for f in range(n):
                    res[a, f, span, cols(r)] = half[f * ROWS : (f + 1) * ROWS]
        tile = bx[me_dp]
        for d in range(n):
            part = jnp.sum(jnp.where(distance == d, total, 0.0), axis=1, keepdims=True)
            part = jnp.sum(part, axis=0, keepdims=True)
            tile = jnp.where((line == r) & (lane == d), part, tile)
        bx[me_dp] = tile

    def step(r, _):
        def pair(i, _):
            for j in range(2):
                spatial(r * n + 2 * i + j)
            return 0

        lax.fori_loop(0, n // 2, pair, 0)
        if n % 2:
            spatial(r * n + n - 1)
        for a in range(4):
            for off in range(1, n):
                forth(r, a, off, partner(n, me, off, True)).wait_recv()
        temporal(r)
        for a in range(4):
            for off in range(n - 1, 0, -1):
                back(r, a, off, me).start()
        return 0

    lax.fori_loop(0, per, step, 0)

    for off in range(1, dp):
        bias_dp(off, me_dp).start()

    def finish(r, _):
        for a in range(4):
            where = cols(me * per + r)
            outs[a][:, where] = (
                space[a, :, where] + res[a, me, :, cols(r)].astype(jnp.float32)
            ).astype(jnp.bfloat16)
        for a in range(4):
            for off in range(1, n):
                source = partner(n, me, off, True)
                back(r, a, off, source).wait_recv()
                where = cols(source * per + r)
                outs[a][:, where] = (
                    space[a, :, where] + ret[a, :, where].astype(jnp.float32)
                ).astype(jnp.bfloat16)
        return 0

    lax.fori_loop(0, per - 1, finish, 0)

    for off in range(1, dp):
        bias_dp(off, partner(dp, me_dp, off, True)).wait_recv()
    summed = bx[0]
    for g in range(1, dp):
        summed = summed + bx[g]
    by[me] = summed * bias_scale
    for off in range(1, n):
        bias_seq(off, me).start()

    finish(per - 1, 0)

    for off in range(1, n):
        bias_seq(off, partner(n, me, off, True)).wait_recv()
    for s in range(n):
        bg_ref[s * per : (s + 1) * per, :] = by[s, 0:per, 0:n]

    def drain(r, _):
        for a in range(4):
            for off in range(1, n):
                forth(r, a, off, me).wait_send()
                back(r, a, off, me).wait_send()
        return 0

    lax.fori_loop(0, per, drain, 0)
    for off in range(1, dp):
        bias_dp(off, me_dp).wait_send()
    for off in range(1, n):
        bias_seq(off, me).wait_send()


def fused(dp, n, queries, keys, values, cotangent, spatial_count, clip_ids, time_bias):
    shape = queries.shape
    rows, width = shape[2:]
    heads = time_bias.shape[0]
    per = heads // n
    flat = jax.ShapeDtypeStruct((rows, width), jnp.bfloat16)
    anywhere = pl.BlockSpec(memory_space=pl.ANY)
    smem = pl.BlockSpec(memory_space=pltpu.SMEM)
    vmem = pl.BlockSpec(memory_space=pltpu.VMEM)
    dma = pltpu.SemaphoreType.DMA
    results = pl.pallas_call(
        functools.partial(kernel, dp, n, heads, 1.0 / math.sqrt(dp * n * rows)),
        out_shape=[flat] * 4 + [jax.ShapeDtypeStruct(time_bias.shape, jnp.float32)],
        in_specs=[anywhere] * 4 + [smem] * 3,
        out_specs=[vmem] * 5,
        scratch_shapes=[
            pltpu.VMEM((4, rows, width), jnp.bfloat16),
            pltpu.VMEM((4, n, rows, width // n), jnp.bfloat16),
            pltpu.VMEM((4, n, rows, width // n), jnp.bfloat16),
            pltpu.VMEM((4, rows, width), jnp.bfloat16),
            pltpu.VMEM((4, rows, width), jnp.float32),
            pltpu.VMEM((dp, 8, 128), jnp.float32),
            pltpu.VMEM((n, 8, 128), jnp.float32),
            dma((4,)),
            dma((4,)),
            dma((per, 4, n - 1)),
            dma((per, 4, n - 1)),
            dma((per, 4, n - 1)),
            dma((per, 4, n - 1)),
            dma((dp - 1,)),
            dma((dp - 1,)),
            dma((n - 1,)),
            dma((n - 1,)),
        ],
        compiler_params=pltpu.CompilerParams(
            collective_id=0, has_side_effects=True, vmem_limit_bytes=40 * 1024 * 1024
        ),
        name="space_time_attention",
    )(
        *(array.reshape(rows, width) for array in (queries, keys, values, cotangent)),
        spatial_count,
        clip_ids,
        time_bias,
    )
    return tuple(array.reshape(shape) for array in results[:4]) + (results[4],)


def on_mesh(dp, n, queries, *rest):
    groups, frames, rows, width = queries.shape
    heads = rest[-1].shape[0]
    fits = groups == 1 and frames == 1 and rows % ROWS == 0 and (width // heads) % 128 == 0
    if fits and n > 1 and dp > 1 and heads % n == 0 and heads // n <= 8 and n <= 8:
        return fused(dp, n, queries, *rest)
    return on_device(queries, *rest)


def solution(mesh):
    return jax.shard_map(
        functools.partial(on_mesh, mesh.shape["dp"], mesh.shape["seq"]),
        mesh=mesh,
        in_specs=(
            P("dp", "seq", None, None),
            P("dp", "seq", None, None),
            P("dp", "seq", None, None),
            P("dp", "seq", None, None),
            P("dp", "seq"),
            P("dp", None),
            P(),
        ),
        out_specs=(
            P("dp", "seq", None, None),
            P("dp", "seq", None, None),
            P("dp", "seq", None, None),
            P("dp", "seq", None, None),
            P(),
        ),
        check_vma=False,
    )
```

profile of v0, /device:TPU:0, one launch (start us, length us, event | category | flops | bytes accessed | tf_op | source)
XLA Modules:
  0.0 60.5 jit_solution(8151884453982544776)
XLA Ops:
  1.3 0.0 copy-start.5
  1.3 0.7 %copy-done.5 = f32[12,4]{0,1:T(4,128)S(1)} copy-done((f32[12,4]{0,1:T(4,128)S(1)}, f32[12,4]{0,1:T(4,128)}, u32[]{:S(2)}) %copy-start.5) | copy-done | bytes 216
  2.0 0.0 copy-start.4
  2.0 0.1 copy.12.bias_ref
  2.1 0.6 copy-done.4
  2.6 0.0 copy-start
  2.6 1.0 %copy-done = bf16[1,1,144,1536]{3,2,1,0:T(8,128)(2,1)S(1)} copy-done((bf16[1,1,144,1536]{3,2,1,0:T(8,128)(2,1)S(1)}, bf16[1,1,144,1536]{3,2,1,0:T(8,128)(2,1)}, u32[]{:S(2)}) %copy-start) | copy-done | bytes 442392
  3.6 0.0 copy-start.1
  3.6 1.0 %copy-done.1 = bf16[1,1,144,1536]{3,2,1,0:T(8,128)(2,1)S(1)} copy-done((bf16[1,1,144,1536]{3,2,1,0:T(8,128)(2,1)S(1)}, bf16[1,1,144,1536]{3,2,1,0:T(8,128)(2,1)}, u32[]{:S(2)}) %copy-start.1) | copy-done | bytes 442392
  4.6 0.0 copy-start.2
  4.6 1.0 %copy-done.2 = bf16[1,1,144,1536]{3,2,1,0:T(8,128)(2,1)S(1)} copy-done((bf16[1,1,144,1536]{3,2,1,0:T(8,128)(2,1)S(1)}, bf16[1,1,144,1536]{3,2,1,0:T(8,128)(2,1)}, u32[]{:S(2)}) %copy-start.2) | copy-done | bytes 442392
  5.7 0.0 copy-start.3
  5.7 1.0 %copy-done.3 = bf16[1,1,144,1536]{3,2,1,0:T(8,128)(2,1)S(1)} copy-done((bf16[1,1,144,1536]{3,2,1,0:T(8,128)(2,1)S(1)}, bf16[1,1,144,1536]{3,2,1,0:T(8,128)(2,1)}, u32[]{:S(2)}) %copy-start.3) | copy-done | bytes 442392
  6.7 50.1 %space_time_attention.1 = (bf16[144,1536]{1,0:T(8,128)(2,1)S(1)}, bf16[144,1536]{1,0:T(8,128)(2,1)S(1)}, bf16[144,1536]{1,0:T(8,128)(2,1)S(1)}, bf16[144,1536]{1,0:T(8,128)(2,1)S(1)}, f32[12,4]{1,0:T(8,128)S(1)}) custom-call(bf16[144,1536]{1,0:T(8,128)(2,1)S(1)} %bitcast.8, bf16[144,1536]{1,0:T(8,128)(2,1)S(1)} %bitcast.9, bf16[144,1536]{1,0:T(8,128)(2,1)S(1)} %bitcast.10, ...), custom_call_target="tpu_custom_call" | custom-call | tf_op jit(solution)/shard_map/space_time_attention/pallas_call | solution.py:389
  56.8 0.7 %copy.13 = f32[12,4]{0,1:T(4,128)} copy(f32[12,4]{1,0:T(8,128)S(1)} %get-tuple-element.19) | data formatting | bytes 384
  57.4 0.8 %copy.19 = bf16[1,1,144,1536]{3,2,1,0:T(8,128)(2,1)} copy(bf16[1,1,144,1536]{3,2,1,0:T(8,128)(2,1)S(1)} %bitcast.15) | data formatting | bytes 884736
  58.2 0.8 %copy.20 = bf16[1,1,144,1536]{3,2,1,0:T(8,128)(2,1)} copy(bf16[1,1,144,1536]{3,2,1,0:T(8,128)(2,1)S(1)} %bitcast.14) | data formatting | bytes 884736
  59.0 0.8 %copy.21 = bf16[1,1,144,1536]{3,2,1,0:T(8,128)(2,1)} copy(bf16[1,1,144,1536]{3,2,1,0:T(8,128)(2,1)S(1)} %bitcast.13) | data formatting | bytes 884736
  59.7 0.8 %copy.22 = bf16[1,1,144,1536]{3,2,1,0:T(8,128)(2,1)} copy(bf16[1,1,144,1536]{3,2,1,0:T(8,128)(2,1)S(1)} %bitcast.12) | data formatting | bytes 884736
Async XLA Ops:
  1.3 0.7 %copy-start.5 = (f32[12,4]{0,1:T(4,128)S(1)}, f32[12,4]{0,1:T(4,128)}, u32[]{:S(2)}) copy-start(f32[12,4]{0,1:T(4,128)} %param.13) | copy-start | bytes 580
  2.0 0.7 %copy-start.4 = (s32[1,4]{1,0:T(1,128)S(1)}, s32[1,4]{1,0:T(1,128)}, u32[]{:S(2)}) copy-start(s32[1,4]{1,0:T(1,128)} %clip_ref.1) | copy-start | bytes 52
  2.6 1.0 %copy-start = (bf16[1,1,144,1536]{3,2,1,0:T(8,128)(2,1)S(1)}, bf16[1,1,144,1536]{3,2,1,0:T(8,128)(2,1)}, u32[]{:S(2)}) copy-start(bf16[1,1,144,1536]{3,2,1,0:T(8,128)(2,1)} %param.7) | copy-start | bytes 1327108
  3.6 1.0 %copy-start.1 = (bf16[1,1,144,1536]{3,2,1,0:T(8,128)(2,1)S(1)}, bf16[1,1,144,1536]{3,2,1,0:T(8,128)(2,1)}, u32[]{:S(2)}) copy-start(bf16[1,1,144,1536]{3,2,1,0:T(8,128)(2,1)} %param.8) | copy-start | bytes 1327108
  4.6 1.0 %copy-start.2 = (bf16[1,1,144,1536]{3,2,1,0:T(8,128)(2,1)S(1)}, bf16[1,1,144,1536]{3,2,1,0:T(8,128)(2,1)}, u32[]{:S(2)}) copy-start(bf16[1,1,144,1536]{3,2,1,0:T(8,128)(2,1)} %param.9) | copy-start | bytes 1327108
  5.7 1.0 %copy-start.3 = (bf16[1,1,144,1536]{3,2,1,0:T(8,128)(2,1)S(1)}, bf16[1,1,144,1536]{3,2,1,0:T(8,128)(2,1)}, u32[]{:S(2)}) copy-start(bf16[1,1,144,1536]{3,2,1,0:T(8,128)(2,1)} %param.10) | copy-start | bytes 1327108
where the time goes:
time: 60.8 us; the launch traced here: 60.5 us
  Pallas kernels  50.1 us (82%)
  local copies, waits for them, and re-layouts  9.09 us (15%)
  between operations  1.3 us (2%)
    pallas_call x1, Pallas kernels, fused(): pl.pallas_call(functools.partial(kernel, dp, n, heads, 1.0 / math.sqrt(dp...  50.1 us
    unnamed x18, local copies, waits for them, and re-layouts  9.09 us

commit v1 on v0

--- a/solution.py
+++ b/solution.py
@@ -126,6 +126,7 @@
 
 
 ROWS = 16
+VMEM_BYTES = 60_000_000
 MESH = pl.DeviceIdType.MESH
 NT = (((1,), (1,)), ((), ()))
 NN = (((1,), (0,)), ((), ()))
@@ -169,8 +170,8 @@
     dp, n, heads, bias_scale,
     q_ref, k_ref, v_ref, c_ref, count_ref, clip_ref, bias_ref,
     out_ref, qg_ref, kg_ref, vg_ref, bg_ref,
-    held, rx, res, ret, space, bx, by,
-    load_sem, own_sem, fs, fr, bs, br, xs, xr, ys, yr,
+    held, rx, res, ret, space, done, bx, by,
+    load_sem, own_sem, fs, fr, bs, br, xs, xr, ys, yr, ws,
 ):
     ins = (q_ref, k_ref, v_ref, c_ref)
     outs = (out_ref, qg_ref, kg_ref, vg_ref)
@@ -247,10 +248,13 @@
         )
     pl.semaphore_wait(barrier, n - 1 + dp - 1)
 
-    for r in range(per):
+    def send(r):
         for a in range(4):
             for off in range(n - 1, 0, -1):
                 forth(r, a, off, me).start()
+
+    for r in range(min(2, per)):
+        send(r)
 
     tokens = n * ROWS
     row = lax.broadcasted_iota(jnp.int32, (tokens, tokens), 0)
@@ -283,7 +287,7 @@
         head = me * per + r
         bias = jnp.zeros((tokens, tokens), jnp.float32)
         for d in range(n):
-            bias = jnp.where(distance == d, bias_ref[head, d], bias)
+            bias = jnp.where(distance == d, bias_ref[d, head], bias)
         extra = jnp.where(allowed, bias, -1e30)
         total = jnp.zeros((tokens, tokens), jnp.float32)
         for b in range(rows // ROWS):
@@ -302,21 +306,24 @@
         for d in range(n):
             part = jnp.sum(jnp.where(distance == d, total, 0.0), axis=1, keepdims=True)
             part = jnp.sum(part, axis=0, keepdims=True)
-            tile = jnp.where((line == r) & (lane == d), part, tile)
+            tile = jnp.where((line == d) & (lane == head), part, tile)
         bx[me_dp] = tile
 
+    def pair(i, _):
+        for j in range(2):
+            spatial(2 * i + j)
+        return 0
+
     def step(r, _):
-        def pair(i, _):
-            for j in range(2):
-                spatial(r * n + 2 * i + j)
-            return 0
-
-        lax.fori_loop(0, n // 2, pair, 0)
-        if n % 2:
-            spatial(r * n + n - 1)
+        lax.fori_loop(r + 1 - 1 // (r + 1), r + 2, pair, 0)
         for a in range(4):
             for off in range(1, n):
                 forth(r, a, off, partner(n, me, off, True)).wait_recv()
+
+        @pl.when(r + 2 < per)
+        def _():
+            send(r + 2)
+
         temporal(r)
         for a in range(4):
             for off in range(n - 1, 0, -1):
@@ -328,20 +335,30 @@
     for off in range(1, dp):
         bias_dp(off, me_dp).start()
 
+    lax.fori_loop(per + 1, heads // 2, pair, 0)
+
+    def write(r, a, off, source):
+        where = cols(source * per + r)
+        return pltpu.make_async_copy(
+            done.at[a, :, where], outs[a].at[:, where], ws.at[r, a, off]
+        )
+
     def finish(r, _):
         for a in range(4):
             where = cols(me * per + r)
-            outs[a][:, where] = (
+            done[a, :, where] = (
                 space[a, :, where] + res[a, me, :, cols(r)].astype(jnp.float32)
             ).astype(jnp.bfloat16)
+            write(r, a, 0, me).start()
         for a in range(4):
             for off in range(1, n):
                 source = partner(n, me, off, True)
                 back(r, a, off, source).wait_recv()
                 where = cols(source * per + r)
-                outs[a][:, where] = (
+                done[a, :, where] = (
                     space[a, :, where] + ret[a, :, where].astype(jnp.float32)
                 ).astype(jnp.bfloat16)
+                write(r, a, off, source).start()
         return 0
 
     lax.fori_loop(0, per - 1, finish, 0)
@@ -359,14 +376,18 @@
 
     for off in range(1, n):
         bias_seq(off, partner(n, me, off, True)).wait_recv()
-    for s in range(n):
-        bg_ref[s * per : (s + 1) * per, :] = by[s, 0:per, 0:n]
+    joined = by[0]
+    for s in range(1, n):
+        joined = joined + by[s]
+    bg_ref[...] = joined[0:n, 0:heads]
 
     def drain(r, _):
         for a in range(4):
             for off in range(1, n):
                 forth(r, a, off, me).wait_send()
                 back(r, a, off, me).wait_send()
+                write(r, a, off, partner(n, me, off, True)).wait()
+            write(r, a, 0, me).wait()
         return 0
 
     lax.fori_loop(0, per, drain, 0)
@@ -374,6 +395,25 @@
         bias_dp(off, me_dp).wait_send()
     for off in range(1, n):
         bias_seq(off, me).wait_send()
+
+
+def hand_over(*refs):
+    count = len(refs) // 2
+    copies = []
+    for i in range(count):
+        rows = refs[i].shape[0]
+        cuts = 3 if rows % (3 * ROWS) == 0 else 1
+        for cut in range(cuts):
+            part = pl.ds(cut * rows // cuts, rows // cuts)
+            copies.append(
+                pltpu.make_async_copy(
+                    refs[i].at[part], refs[count + i].at[part], refs[-1].at[i, cut]
+                )
+            )
+    for copy in copies:
+        copy.start()
+    for copy in copies:
+        copy.wait()
 
 
 def fused(dp, n, queries, keys, values, cotangent, spatial_count, clip_ids, time_bias):
@@ -382,21 +422,23 @@
     heads = time_bias.shape[0]
     per = heads // n
     flat = jax.ShapeDtypeStruct((rows, width), jnp.bfloat16)
-    anywhere = pl.BlockSpec(memory_space=pl.ANY)
+    hbm = pl.BlockSpec(memory_space=pltpu.HBM)
     smem = pl.BlockSpec(memory_space=pltpu.SMEM)
     vmem = pl.BlockSpec(memory_space=pltpu.VMEM)
     dma = pltpu.SemaphoreType.DMA
+    shapes = [flat] * 4 + [jax.ShapeDtypeStruct((n, heads), jnp.float32)]
     results = pl.pallas_call(
         functools.partial(kernel, dp, n, heads, 1.0 / math.sqrt(dp * n * rows)),
-        out_shape=[flat] * 4 + [jax.ShapeDtypeStruct(time_bias.shape, jnp.float32)],
-        in_specs=[anywhere] * 4 + [smem] * 3,
-        out_specs=[vmem] * 5,
+        out_shape=shapes,
+        in_specs=[hbm] * 4 + [smem] * 3,
+        out_specs=[hbm] * 4 + [vmem],
         scratch_shapes=[
             pltpu.VMEM((4, rows, width), jnp.bfloat16),
             pltpu.VMEM((4, n, rows, width // n), jnp.bfloat16),
             pltpu.VMEM((4, n, rows, width // n), jnp.bfloat16),
             pltpu.VMEM((4, rows, width), jnp.bfloat16),
             pltpu.VMEM((4, rows, width), jnp.float32),
+            pltpu.VMEM((4, rows, width), jnp.bfloat16),
             pltpu.VMEM((dp, 8, 128), jnp.float32),
             pltpu.VMEM((n, 8, 128), jnp.float32),
             dma((4,)),
@@ -409,25 +451,35 @@
             dma((dp - 1,)),
             dma((n - 1,)),
             dma((n - 1,)),
+            dma((per, 4, n)),
         ],
         compiler_params=pltpu.CompilerParams(
-            collective_id=0, has_side_effects=True, vmem_limit_bytes=40 * 1024 * 1024
+            collective_id=0, has_side_effects=True, vmem_limit_bytes=VMEM_BYTES
         ),
         name="space_time_attention",
     )(
         *(array.reshape(rows, width) for array in (queries, keys, values, cotangent)),
         spatial_count,
         clip_ids,
-        time_bias,
-    )
-    return tuple(array.reshape(shape) for array in results[:4]) + (results[4],)
+        time_bias.T,
+    )
+    results = pl.pallas_call(
+        hand_over,
+        out_shape=shapes,
+        in_specs=[hbm] * 5,
+        out_specs=[hbm] * 5,
+        scratch_shapes=[dma((5, 3))],
+        compiler_params=pltpu.CompilerParams(vmem_limit_bytes=VMEM_BYTES),
+        name="hand_over",
+    )(*results)
+    return tuple(array.reshape(shape) for array in results[:4]) + (results[4].T,)
 
 
 def on_mesh(dp, n, queries, *rest):
     groups, frames, rows, width = queries.shape
     heads = rest[-1].shape[0]
     fits = groups == 1 and frames == 1 and rows % ROWS == 0 and (width // heads) % 128 == 0
-    if fits and n > 1 and dp > 1 and heads % n == 0 and heads // n <= 8 and n <= 8:
+    if fits and heads <= 128 and n > 1 and dp > 1 and heads % n == 0 and heads % 2 == 0 and heads // n < heads // 2 and n <= 8:
         return fused(dp, n, queries, *rest)
     return on_device(queries, *rest)
 

time: 60.8 us -> 107 us (1.76)
  Pallas kernels: 50.1 us -> 105 us
  local copies, waits for them, and re-layouts: 9.09 us -> 0 us
    pallas_call x0 -> x1, Pallas kernels: none -> 54.9 us  [fused(): pl.pallas_call(hand_over, out_shape=shapes, in_specs=[hbm] * 5, out_specs...]
    unnamed x18 -> x0, local copies, waits for them, and re-layouts: 9.09 us -> none
where the time goes in v1:
time: 107 us
  Pallas kernels  105 us (98%)
  between operations  1.29 us (1%)
    pallas_call x1, Pallas kernels, fused(): pl.pallas_call(hand_over, out_shape=shapes, in_specs=[hbm] * 5, out_specs...  54.9 us
    pallas_call x1, Pallas kernels, fused(): pl.pallas_call(functools.partial(kernel, dp, n, heads, 1.0 / math.sqrt(dp...  50.4 us

profile of v1, /device:TPU:0, one launch (start us, length us, event | category | flops | bytes accessed | tf_op | source)
XLA Modules:
  0.0 106.6 jit_solution(2722125516062948226)
XLA Ops:
  1.3 50.4 %space_time_attention.1 = (bf16[144,1536]{1,0:T(8,128)(2,1)}, bf16[144,1536]{1,0:T(8,128)(2,1)}, bf16[144,1536]{1,0:T(8,128)(2,1)}, bf16[144,1536]{1,0:T(8,128)(2,1)}, f32[4,12]{1,0:T(4,128)}) custom-call(bf16[144,1536]{1,0:T(8,128)(2,1)} %bitcast.10, bf16[144,1536]{1,0:T(8,128)(2,1)} %bitcast.11, bf16[144,1536]{1,0:T(8,128)(2,1)} %bitcast.12, ...), custom_call_target="tpu_custom_call" | custom-call | tf_op jit(solution)/shard_map/space_time_attention/pallas_call | solution.py:430
  51.7 54.9 %hand_over.1 = (bf16[144,1536]{1,0:T(8,128)(2,1)}, bf16[144,1536]{1,0:T(8,128)(2,1)}, bf16[144,1536]{1,0:T(8,128)(2,1)}, bf16[144,1536]{1,0:T(8,128)(2,1)}, f32[4,12]{1,0:T(4,128)}) custom-call(bf16[144,1536]{1,0:T(8,128)(2,1)} %get-tuple-element.15.refs_0_, bf16[144,1536]{1,0:T(8,128)(2,1)} %get-tuple-element.16.refs_1_, ...), custom_call_target="tpu_custom_call" | custom-call | tf_op jit(solution)/shard_map/hand_over/pallas_call | solution.py:466

commit v2 on v1

--- a/solution.py
+++ b/solution.py
@@ -398,21 +398,24 @@
 
 
 def hand_over(*refs):
-    count = len(refs) // 2
-    copies = []
+    count = (len(refs) - 2) // 3
+    sources, targets, stages = refs[:count], refs[count : 2 * count], refs[2 * count : 3 * count]
+    into_sem, out_sem = refs[3 * count :]
+    into, out = [], []
     for i in range(count):
-        rows = refs[i].shape[0]
+        rows = sources[i].shape[0]
         cuts = 3 if rows % (3 * ROWS) == 0 else 1
         for cut in range(cuts):
             part = pl.ds(cut * rows // cuts, rows // cuts)
-            copies.append(
-                pltpu.make_async_copy(
-                    refs[i].at[part], refs[count + i].at[part], refs[-1].at[i, cut]
-                )
-            )
-    for copy in copies:
+            stage = stages[i].at[part]
+            into.append(pltpu.make_async_copy(sources[i].at[part], stage, into_sem.at[i, cut]))
+            out.append(pltpu.make_async_copy(stage, targets[i].at[part], out_sem.at[i, cut]))
+    for copy in into:
         copy.start()
-    for copy in copies:
+    for here, there in zip(into, out):
+        here.wait()
+        there.start()
+    for copy in out:
         copy.wait()
 
 
@@ -468,7 +471,8 @@
         out_shape=shapes,
         in_specs=[hbm] * 5,
         out_specs=[hbm] * 5,
-        scratch_shapes=[dma((5, 3))],
+        scratch_shapes=[pltpu.VMEM(kind.shape, kind.dtype) for kind in shapes]
+        + [dma((5, 3)), dma((5, 3))],
         compiler_params=pltpu.CompilerParams(vmem_limit_bytes=VMEM_BYTES),
         name="hand_over",
     )(*results)

time: 107 us -> 54.3 us (0.51)
  Pallas kernels: 105 us -> 52.9 us
    pallas_call x1, Pallas kernels: 54.9 us -> 2.47 us  [fused(): pl.pallas_call(hand_over, out_shape=shapes, in_specs=[hbm] * 5, out_specs...]
where the time goes in v2:
time: 54.3 us; the launch traced here: 54.2 us
  Pallas kernels  52.9 us (97%)
  between operations  1.29 us (2%)
    pallas_call x1, Pallas kernels, fused(): pl.pallas_call(functools.partial(kernel, dp, n, heads, 1.0 / math.sqrt(dp...  50.4 us
    pallas_call x1, Pallas kernels, fused(): pl.pallas_call(hand_over, out_shape=shapes, in_specs=[hbm] * 5, out_specs...  2.47 us

profile of v2, /device:TPU:0, one launch (start us, length us, event | category | flops | bytes accessed | tf_op | source)
XLA Modules:
  0.0 54.2 jit_solution(7833070755558458235)
XLA Ops:
  1.3 50.4 %space_time_attention.1 = (bf16[144,1536]{1,0:T(8,128)(2,1)}, bf16[144,1536]{1,0:T(8,128)(2,1)}, bf16[144,1536]{1,0:T(8,128)(2,1)}, bf16[144,1536]{1,0:T(8,128)(2,1)}, f32[4,12]{1,0:T(4,128)}) custom-call(bf16[144,1536]{1,0:T(8,128)(2,1)} %bitcast.10, bf16[144,1536]{1,0:T(8,128)(2,1)} %bitcast.11, bf16[144,1536]{1,0:T(8,128)(2,1)} %bitcast.12, ...), custom_call_target="tpu_custom_call" | custom-call | tf_op jit(solution)/shard_map/space_time_attention/pallas_call | solution.py:433
  51.7 2.5 %hand_over.1 = (bf16[144,1536]{1,0:T(8,128)(2,1)}, bf16[144,1536]{1,0:T(8,128)(2,1)}, bf16[144,1536]{1,0:T(8,128)(2,1)}, bf16[144,1536]{1,0:T(8,128)(2,1)}, f32[4,12]{1,0:T(4,128)}) custom-call(bf16[144,1536]{1,0:T(8,128)(2,1)} %get-tuple-element.15.refs_0_, bf16[144,1536]{1,0:T(8,128)(2,1)} %get-tuple-element.16.refs_1_, ...), custom_call_target="tpu_custom_call" | custom-call | tf_op jit(solution)/shard_map/hand_over/pallas_call | solution.py:469

commit v3 on v2

--- a/solution.py
+++ b/solution.py
@@ -256,17 +256,22 @@
     for r in range(min(2, per)):
         send(r)
 
-    tokens = n * ROWS
-    row = lax.broadcasted_iota(jnp.int32, (tokens, tokens), 0)
-    col = lax.broadcasted_iota(jnp.int32, (tokens, tokens), 1)
-    row_frame, col_frame = row // ROWS, col // ROWS
-    distance = jnp.abs(row_frame - col_frame)
-    row_clip = jnp.zeros((tokens, tokens), jnp.int32)
-    col_clip = jnp.zeros((tokens, tokens), jnp.int32)
-    for f in range(n):
-        row_clip = jnp.where(row_frame == f, clip_ref[0, f], row_clip)
-        col_clip = jnp.where(col_frame == f, clip_ref[0, f], col_clip)
-    allowed = (row_clip == col_clip) & (row - row_frame * ROWS == col - col_frame * ROWS)
+    def pairs_of(span):
+        tokens = n * span
+        row = lax.broadcasted_iota(jnp.int32, (tokens, tokens), 0)
+        col = lax.broadcasted_iota(jnp.int32, (tokens, tokens), 1)
+        row_frame, col_frame = row // span, col // span
+        row_clip = jnp.zeros((tokens, tokens), jnp.int32)
+        col_clip = jnp.zeros((tokens, tokens), jnp.int32)
+        for f in range(n):
+            row_clip = jnp.where(row_frame == f, clip_ref[0, f], row_clip)
+            col_clip = jnp.where(col_frame == f, clip_ref[0, f], col_clip)
+        same = row - row_frame * span == col - col_frame * span
+        return jnp.abs(row_frame - col_frame), (row_clip == col_clip) & same
+
+    wide = max(ROWS, 128 // n // ROWS * ROWS)
+    spans = [(at, min(wide, rows - at)) for at in range(0, rows, wide)]
+    pairs = {span: pairs_of(span) for _, span in spans}
     live = lax.broadcasted_iota(jnp.int32, (rows, rows), 1) < count_ref[0, 0]
     space_extra = jnp.where(live, 0.0, -1e30)
     lane = lax.broadcasted_iota(jnp.int32, (8, 128), 1)
@@ -285,27 +290,32 @@
 
     def temporal(r):
         head = me * per + r
-        bias = jnp.zeros((tokens, tokens), jnp.float32)
-        for d in range(n):
-            bias = jnp.where(distance == d, bias_ref[d, head], bias)
-        extra = jnp.where(allowed, bias, -1e30)
-        total = jnp.zeros((tokens, tokens), jnp.float32)
-        for b in range(rows // ROWS):
-            span = pl.ds(b * ROWS, ROWS)
+        extras, totals = {}, {}
+        for span, (distance, allowed) in pairs.items():
+            bias = jnp.zeros(distance.shape, jnp.float32)
+            for d in range(n):
+                bias = jnp.where(distance == d, bias_ref[d, head], bias)
+            extras[span] = jnp.where(allowed, bias, -1e30)
+            totals[span] = jnp.zeros(distance.shape, jnp.float32)
+        for at, span in spans:
             parts = [
-                jnp.concatenate([rx[a, f, span, cols(r)] for f in range(n)], axis=0)
+                jnp.concatenate([rx[a, f, at : at + span, cols(r)] for f in range(n)], axis=0)
                 for a in range(4)
             ]
-            grads, score_grad = attend_block(*parts, extra, scaling)
-            total = total + score_grad
+            grads, score_grad = attend_block(*parts, extras[span], scaling)
+            totals[span] = totals[span] + score_grad
             for a in range(4):
                 half = grads[a].astype(jnp.bfloat16)
                 for f in range(n):
-                    res[a, f, span, cols(r)] = half[f * ROWS : (f + 1) * ROWS]
+                    res[a, f, at : at + span, cols(r)] = half[f * span : (f + 1) * span]
         tile = bx[me_dp]
         for d in range(n):
-            part = jnp.sum(jnp.where(distance == d, total, 0.0), axis=1, keepdims=True)
-            part = jnp.sum(part, axis=0, keepdims=True)
+            part = jnp.zeros((1, 1), jnp.float32)
+            for span, (distance, _) in pairs.items():
+                one = jnp.sum(
+                    jnp.where(distance == d, totals[span], 0.0), axis=1, keepdims=True
+                )
+                part = part + jnp.sum(one, axis=0, keepdims=True)
             tile = jnp.where((line == d) & (lane == head), part, tile)
         bx[me_dp] = tile
 
@@ -315,7 +325,6 @@
         return 0
 
     def step(r, _):
-        lax.fori_loop(r + 1 - 1 // (r + 1), r + 2, pair, 0)
         for a in range(4):
             for off in range(1, n):
                 forth(r, a, off, partner(n, me, off, True)).wait_recv()
@@ -330,12 +339,14 @@
                 back(r, a, off, me).start()
         return 0
 
+    early = heads // 4
+    lax.fori_loop(0, early, pair, 0)
     lax.fori_loop(0, per, step, 0)
 
     for off in range(1, dp):
         bias_dp(off, me_dp).start()
 
-    lax.fori_loop(per + 1, heads // 2, pair, 0)
+    lax.fori_loop(early, heads // 2, pair, 0)
 
     def write(r, a, off, source):
         where = cols(source * per + r)
@@ -483,7 +494,7 @@
     groups, frames, rows, width = queries.shape
     heads = rest[-1].shape[0]
     fits = groups == 1 and frames == 1 and rows % ROWS == 0 and (width // heads) % 128 == 0
-    if fits and heads <= 128 and n > 1 and dp > 1 and heads % n == 0 and heads % 2 == 0 and heads // n < heads // 2 and n <= 8:
+    if fits and heads <= 128 and n > 1 and dp > 1 and heads % n == 0 and heads % 2 == 0 and n <= 8:
         return fused(dp, n, queries, *rest)
     return on_device(queries, *rest)
 

time: 54.3 us -> 54.3 us (level)
  no operation moved by 1% of the time
where the time goes in v3:
time: 54.3 us; the launch traced here: 54.2 us
  Pallas kernels  52.9 us (97%)
  between operations  1.29 us (2%)
    pallas_call x1, Pallas kernels, fused(): pl.pallas_call(functools.partial(kernel, dp, n, heads, 1.0 / math.sqrt(dp...  50.4 us
    pallas_call x1, Pallas kernels, fused(): pl.pallas_call(hand_over, out_shape=shapes, in_specs=[hbm] * 5, out_specs...  2.47 us

profile of v3, /device:TPU:0, one launch (start us, length us, event | category | flops | bytes accessed | tf_op | source)
XLA Modules:
  0.0 54.2 jit_solution(1716568190922972557)
XLA Ops:
  1.3 50.4 %space_time_attention.1 = (bf16[144,1536]{1,0:T(8,128)(2,1)}, bf16[144,1536]{1,0:T(8,128)(2,1)}, bf16[144,1536]{1,0:T(8,128)(2,1)}, bf16[144,1536]{1,0:T(8,128)(2,1)}, f32[4,12]{1,0:T(4,128)}) custom-call(bf16[144,1536]{1,0:T(8,128)(2,1)} %bitcast.10, bf16[144,1536]{1,0:T(8,128)(2,1)} %bitcast.11, bf16[144,1536]{1,0:T(8,128)(2,1)} %bitcast.12, ...), custom_call_target="tpu_custom_call" | custom-call | tf_op jit(solution)/shard_map/space_time_attention/pallas_call | solution.py:444
  51.7 2.5 %hand_over.1 = (bf16[144,1536]{1,0:T(8,128)(2,1)}, bf16[144,1536]{1,0:T(8,128)(2,1)}, bf16[144,1536]{1,0:T(8,128)(2,1)}, bf16[144,1536]{1,0:T(8,128)(2,1)}, f32[4,12]{1,0:T(4,128)}) custom-call(bf16[144,1536]{1,0:T(8,128)(2,1)} %get-tuple-element.15.refs_0_, bf16[144,1536]{1,0:T(8,128)(2,1)} %get-tuple-element.16.refs_1_, ...), custom_call_target="tpu_custom_call" | custom-call | tf_op jit(solution)/shard_map/hand_over/pallas_call | solution.py:480

commit v4 on v3

--- a/solution.py
+++ b/solution.py
@@ -214,15 +214,32 @@
             device_id_type=MESH,
         )
 
-    def bias_dp(off, slot):
+    def pass_on(way, s, slot):
         return pltpu.make_async_remote_copy(
-            src_ref=bx.at[me_dp],
+            src_ref=bx.at[slot],
             dst_ref=bx.at[slot],
-            send_sem=xs.at[off - 1],
-            recv_sem=xr.at[off - 1],
-            device_id={"dp": partner(dp, me_dp, off)},
+            send_sem=xs.at[way, s],
+            recv_sem=xr.at[way, s],
+            device_id={"dp": me_dp - 1 if way else me_dp + 1},
             device_id_type=MESH,
         )
+
+    def line_step(s):
+        @pl.when((me_dp < dp - 1) & (me_dp >= s))
+        def _():
+            pass_on(0, s, me_dp - s).start()
+
+        @pl.when((me_dp > 0) & (me_dp + s < dp))
+        def _():
+            pass_on(1, s, me_dp + s).start()
+
+        @pl.when(me_dp >= s + 1)
+        def _():
+            pass_on(0, s, me_dp - 1 - s).wait_recv()
+
+        @pl.when(me_dp + 1 + s < dp)
+        def _():
+            pass_on(1, s, me_dp + 1 + s).wait_recv()
 
     def bias_seq(off, slot):
         return pltpu.make_async_remote_copy(
@@ -242,11 +259,16 @@
         pl.semaphore_signal(
             barrier, inc=1, device_id={"seq": partner(n, me, off)}, device_id_type=MESH
         )
-    for off in range(1, dp):
-        pl.semaphore_signal(
-            barrier, inc=1, device_id={"dp": partner(dp, me_dp, off)}, device_id_type=MESH
-        )
-    pl.semaphore_wait(barrier, n - 1 + dp - 1)
+    for there, step_to in ((me_dp > 0, -1), (me_dp < dp - 1, 1)):
+
+        @pl.when(there)
+        def _():
+            pl.semaphore_signal(
+                barrier, inc=1, device_id={"dp": me_dp + step_to}, device_id_type=MESH
+            )
+
+    ends = 1 // (me_dp + 1) + (me_dp + 1) // dp
+    pl.semaphore_wait(barrier, n + 1 - ends)
 
     def send(r):
         for a in range(4):
@@ -343,9 +365,6 @@
     lax.fori_loop(0, early, pair, 0)
     lax.fori_loop(0, per, step, 0)
 
-    for off in range(1, dp):
-        bias_dp(off, me_dp).start()
-
     lax.fori_loop(early, heads // 2, pair, 0)
 
     def write(r, a, off, source):
@@ -372,10 +391,12 @@
                 write(r, a, off, source).start()
         return 0
 
+    half = (dp - 1) // 2
+    for s in range(half):
+        line_step(s)
     lax.fori_loop(0, per - 1, finish, 0)
-
-    for off in range(1, dp):
-        bias_dp(off, partner(dp, me_dp, off, True)).wait_recv()
+    for s in range(half, dp - 1):
+        line_step(s)
     summed = bx[0]
     for g in range(1, dp):
         summed = summed + bx[g]
@@ -402,8 +423,16 @@
         return 0
 
     lax.fori_loop(0, per, drain, 0)
-    for off in range(1, dp):
-        bias_dp(off, me_dp).wait_send()
+    for s in range(dp - 1):
+
+        @pl.when((me_dp < dp - 1) & (me_dp >= s))
+        def _():
+            pass_on(0, s, me_dp - s).wait_send()
+
+        @pl.when((me_dp > 0) & (me_dp + s < dp))
+        def _():
+            pass_on(1, s, me_dp + s).wait_send()
+
     for off in range(1, n):
         bias_seq(off, me).wait_send()
 
@@ -461,8 +490,8 @@
             dma((per, 4, n - 1)),
             dma((per, 4, n - 1)),
             dma((per, 4, n - 1)),
-            dma((dp - 1,)),
-            dma((dp - 1,)),
+            dma((2, dp - 1)),
+            dma((2, dp - 1)),
             dma((n - 1,)),
             dma((n - 1,)),
             dma((per, 4, n)),

time: 54.3 us -> 56.3 us (1.037)
  Pallas kernels: 52.9 us -> 54.8 us
    pallas_call x1, Pallas kernels: 50.4 us -> 52.4 us  [fused(): pl.pallas_call(functools.partial(kernel, dp, n, heads, 1.0 / math.sqrt(dp...]
where the time goes in v4:
time: 56.3 us; the launch traced here: 56.1 us
  Pallas kernels  54.8 us (97%)
  between operations  1.29 us (2%)
    pallas_call x1, Pallas kernels, fused(): pl.pallas_call(functools.partial(kernel, dp, n, heads, 1.0 / math.sqrt(dp...  52.4 us
    pallas_call x1, Pallas kernels, fused(): pl.pallas_call(hand_over, out_shape=shapes, in_specs=[hbm] * 5, out_specs...  2.47 us

profile of v4, /device:TPU:0, one launch (start us, length us, event | category | flops | bytes accessed | tf_op | source)
XLA Modules:
  0.0 56.1 jit_solution(14691188270552739368)
XLA Ops:
  1.3 52.4 %space_time_attention.1 = (bf16[144,1536]{1,0:T(8,128)(2,1)}, bf16[144,1536]{1,0:T(8,128)(2,1)}, bf16[144,1536]{1,0:T(8,128)(2,1)}, bf16[144,1536]{1,0:T(8,128)(2,1)}, f32[4,12]{1,0:T(4,128)}) custom-call(bf16[144,1536]{1,0:T(8,128)(2,1)} %bitcast.10, bf16[144,1536]{1,0:T(8,128)(2,1)} %bitcast.11, bf16[144,1536]{1,0:T(8,128)(2,1)} %bitcast.12, ...), custom_call_target="tpu_custom_call" | custom-call | tf_op jit(solution)/shard_map/space_time_attention/pallas_call | solution.py:473
  53.7 2.5 %hand_over.1 = (bf16[144,1536]{1,0:T(8,128)(2,1)}, bf16[144,1536]{1,0:T(8,128)(2,1)}, bf16[144,1536]{1,0:T(8,128)(2,1)}, bf16[144,1536]{1,0:T(8,128)(2,1)}, f32[4,12]{1,0:T(4,128)}) custom-call(bf16[144,1536]{1,0:T(8,128)(2,1)} %get-tuple-element.15.refs_0_, bf16[144,1536]{1,0:T(8,128)(2,1)} %get-tuple-element.16.refs_1_, ...), custom_call_target="tpu_custom_call" | custom-call | tf_op jit(solution)/shard_map/hand_over/pallas_call | solution.py:509
